TPU v7x, 256 devices: a whole 4x4x8 slice. The times are simulated.
256 devices in a mesh: conf: 64 (over z, x, core), state: 4 (over y).
Axes of the slice: x: 4, y: 4, z: 8, core: 2. Of those that a mesh axis runs over, the one named last changes fastest.
Arguments:
- energies: float32 [4096, 131072], P('state', 'conf'), may hold values from -160 to 160
- samples: int32 [4096], P('state'), may hold values from 1 to 63
- counts: int32 [32, 131072], P(None, 'conf'), may hold values from 0 to 2
- initial: float32 [32, 4096], P(None, 'state'), may hold values from -160 to 160
Outputs:
- free_energy: float32 [32, 4096], P(None, 'state')
- log_weight: float32 [32, 131072], P(None, 'conf')
All inputs are finite; a program needn't handle non-finite values.
Results may differ from a plain program's by a relative error of at most 0.0003.
Values sent between devices are 32-bit elements; how exact they have to be, the bound alone decides.
A program may use at most 64 MiB of HBM per device.

v0:
```python
import jax
import jax.numpy as jnp
from jax import lax
from jax.sharding import PartitionSpec as P

ITERS = 2


def spread(block, axis, owner):
    block = jnp.where(lax.axis_index(axis) == owner, block, jnp.zeros_like(block))
    return lax.psum(block, axis)


def per_device(energies, samples, counts, initial):
    shift = lax.pmax(jnp.max(-energies, axis=0), "state")
    boltz = jnp.exp(-energies - shift[None, :])
    log_samples = jnp.log(samples.astype(jnp.float32))
    weight = counts.astype(jnp.float32)
    free = initial
    denom = jnp.ones(weight.shape, jnp.float32)
    top = jnp.zeros((weight.shape[0],), jnp.float32)
    for step in range(ITERS):
        lifted = log_samples[None, :] + free
        top = lax.pmax(jnp.max(lifted, axis=1), "state")
        scaled = jnp.exp(lifted - top[:, None])
        partial_den = jnp.dot(scaled, boltz, precision=lax.Precision.HIGHEST)
        denom = lax.psum(partial_den, "state")
        ratio = weight / denom
        terms = lax.dot_general(
            ratio, boltz, (((1,), (1,)), ((), ())), precision=lax.Precision.HIGHEST
        )
        total = lax.psum(terms, "conf")
        value = top[:, None] - jnp.log(total)
        anchor = spread(value[:, 0], "state", 0)
        free = value - anchor[:, None]
    log_weight = jnp.log(denom) + top[:, None]
    return (free, log_weight)


def solution(mesh):
    in_specs = (P("state", "conf"), P("state"), P(None, "conf"), P(None, "state"))
    out_specs = (P(None, "state"), P(None, "conf"))
    return jax.shard_map(
        per_device, mesh=mesh, in_specs=in_specs, out_specs=out_specs, check_vma=False
    )
```

profile of v0, /device:TPU:1, one launch (start us, length us, event | category | flops | bytes accessed | tf_op | source)
XLA Modules:
  0.0 542.4 jit_solution(7028632906117369752)
XLA Ops:
  7.2 0.0 copy-start.3
  7.2 0.0 copy-start.2
  7.2 0.0 copy-start
  7.2 0.0 all-reduce.6.cloned.1.call-start
  7.2 4.1 negate_reduce_fusion
  11.3 0.0 copy-done.3
  11.3 0.0 copy-done.2
  11.3 0.1 add_reduce_fusion
  11.5 9.8 %all-reduce = (f32[2048]{0:T(1024)S(1)}, f32[32]{0:T(128)S(1)}) all-reduce(f32[2048]{0:T(1024)S(1)} %negate_reduce_fusion, f32[32]{0:T(128)S(1)} %add_reduce_fusion), channel_id=1, replica_groups=mesh['conf'=64,'state'=4] {'state'}, use_global_device_ids=true, to_apply=%region_3.0 | all-reduce | flops 2080 | bytes 16640 | tf_op jit(solution)/shard_map/pmax | solution.py:15
  21.3 8.9 %fusion.3 = f32[32,2048]{1,0:T(8,128)} fusion(f32[1024,2048]{1,0:T(8,128)} %param.4, f32[2048]{0:T(1024)S(1)} %get-tuple-element.2, f32[32,1024]{1,0:T(8,128)S(1)} %copy-done.2, f32[32]{0:T(128)S(1)} %get-tuple-element.3, f32[1024]{0:T(1024)S(1)} %convert_log_fusion), kind=kOutput, calls=%fused_computation.5 | convolution fusion | flops 809566208 | bytes 8794240 | tf_op jit(solution)/shard_map/dot_general | solution.py:26
  30.1 0.0 all-reduce.6.cloned.1.call-update
  30.1 0.0 all-reduce.8.cloned.1.call-start
  30.2 47.4 %all-reduce.6.cloned.1.call-done = f32[32,2048]{1,0:T(8,128)} async-done(((f32[32,2048]{1,0:T(8,128)}), f32[32,2048]{1,0:T(8,128)}) %all-reduce.6.cloned.1.call-update) | async-done | bytes 262160 | tf_op jit(solution)/shard_map/psum | solution.py:27
  77.6 0.0 copy-done
  77.6 12.1 %fusion.2 = f32[32,1024]{1,0:T(8,128)} fusion(f32[1024,2048]{1,0:T(8,128)} %param.4, f32[2048]{0:T(1024)S(1)} %get-tuple-element.2, f32[32,2048]{1,0:T(8,128)} %all-reduce.6.cloned.1.call-done, s32[32,2048]{1,0:T(8,128)S(1)} %copy-done), kind=kOutput, calls=%fused_computation.4 | convolution fusion | flops 809631744 | bytes 9052160 | tf_op jit(solution)/shard_map/dot_general | solution.py:29
  89.7 0.0 all-reduce.8.cloned.1.call-update
  89.8 0.0 all-reduce.10.cloned.1.call-start
  89.8 176.0 %all-reduce.8.cloned.1.call-done = f32[32,1024]{1,0:T(8,128)} async-done(((f32[32,1024]{1,0:T(8,128)}), f32[32,1024]{1,0:T(8,128)}) %all-reduce.8.cloned.1.call-update) | async-done | bytes 131088 | tf_op jit(solution)/shard_map/psum | solution.py:32
  265.8 1.0 log_subtract_fusion.1
  266.8 0.1 fusion.20
  266.9 8.5 %psum.44 = f32[32]{0:T(128)S(1)} all-reduce(f32[32]{0:T(128)S(1)} %fusion.20), channel_id=1, replica_groups=mesh['conf'=64,'state'=4] {'state'}, use_global_device_ids=true, to_apply=%region_6.7 | all-reduce | flops 32 | bytes 256 | tf_op jit(solution)/shard_map/psum | solution.py:11
  275.4 1.1 fusion.13
  276.5 6.2 %pmax.23 = f32[32]{0:T(128)S(1)} all-reduce(f32[32]{0:T(128)S(1)} %fusion.13), channel_id=1, replica_groups=mesh['conf'=64,'state'=4] {'state'}, use_global_device_ids=true, to_apply=%region_8.9 | all-reduce | flops 32 | bytes 256 | tf_op jit(solution)/shard_map/pmax | solution.py:24
  282.6 8.9 %fusion.1 = f32[32,2048]{1,0:T(8,128)} fusion(f32[1024,2048]{1,0:T(8,128)} %param.4, f32[2048]{0:T(1024)S(1)} %get-tuple-element.2, f32[32,1024]{1,0:T(8,128)S(1)} %log_subtract_fusion.1, f32[32]{0:T(128)S(1)} %pmax.23, f32[32]{0:T(128)S(1)} %psum.44, f32[1024]{0:T(1024)S(1)} %convert_log_fusion), kind=kOutput, calls=%fused_computation.3 | convolution fusion | flops 809598976 | bytes 8794368 | tf_op jit(solution)/shard_map/dot_general | solution.py:26
  291.5 0.0 all-reduce.10.cloned.1.call-update
  291.6 0.0 all-reduce.12.cloned.1.call-start
  291.6 44.8 %all-reduce.10.cloned.1.call-done = f32[32,2048]{1,0:T(8,128)} async-done(((f32[32,2048]{1,0:T(8,128)}), f32[32,2048]{1,0:T(8,128)}) %all-reduce.10.cloned.1.call-update) | async-done | bytes 262160 | tf_op jit(solution)/shard_map/psum | solution.py:27
  336.4 0.0 copy-start.1
  336.4 12.1 %fusion = f32[32,1024]{1,0:T(8,128)} fusion(f32[1024,2048]{1,0:T(8,128)} %param.4, f32[2048]{0:T(1024)S(1)} %get-tuple-element.2, f32[32,2048]{1,0:T(8,128)} %all-reduce.10.cloned.1.call-done, s32[32,2048]{1,0:T(8,128)S(1)} %copy-done), kind=kOutput, calls=%fused_computation.2 | convolution fusion | flops 809631744 | bytes 9052160 | tf_op jit(solution)/shard_map/dot_general | solution.py:29
  348.6 0.0 all-reduce.12.cloned.1.call-update
  348.6 0.0 copy-done.1
  348.6 0.8 log_add_fusion
  349.4 175.3 %all-reduce.12.cloned.1.call-done = f32[32,1024]{1,0:T(8,128)} async-done(((f32[32,1024]{1,0:T(8,128)}), f32[32,1024]{1,0:T(8,128)}) %all-reduce.12.cloned.1.call-update) | async-done | bytes 131088 | tf_op jit(solution)/shard_map/psum | solution.py:32
  524.7 1.0 log_subtract_fusion
  525.7 0.1 fusion.19
  525.8 8.5 %psum.47 = f32[32]{0:T(128)S(1)} all-reduce(f32[32]{0:T(128)S(1)} %fusion.19), channel_id=1, replica_groups=mesh['conf'=64,'state'=4] {'state'}, use_global_device_ids=true, to_apply=%region_11.12 | all-reduce | flops 32 | bytes 256 | tf_op jit(solution)/shard_map/psum | solution.py:11
  534.2 1.6 broadcast_subtract_fusion
  (1 shorter events, 0.0 us)
Async XLA Ops:
  7.2 4.1 copy-start.3
  7.2 4.2 copy-start.2
  7.2 70.4 %copy-start = (s32[32,2048]{1,0:T(8,128)S(1)}, s32[32,2048]{1,0:T(8,128)}, u32[]{:S(2)}) copy-start(s32[32,2048]{1,0:T(8,128)} %param.6) | copy-start | bytes 786436
  7.2 70.4 %all-reduce.6.cloned.1.call-start = ((), (), s32[]{:S(2)}) async-start(), calls=%async_computation | async-start | bytes 524288 | tf_op jit(solution)/shard_map/psum | solution.py:27
  30.1 235.7 %all-reduce.8.cloned.1.call-start = ((), (), s32[]{:S(2)}) async-start(), calls=%async_computation.1 | async-start | bytes 262144 | tf_op jit(solution)/shard_map/psum | solution.py:32
  89.8 246.6 %all-reduce.10.cloned.1.call-start = ((), (), s32[]{:S(2)}) async-start(), calls=%async_computation.2 | async-start | bytes 524288 | tf_op jit(solution)/shard_map/psum | solution.py:27
  291.6 233.1 %all-reduce.12.cloned.1.call-start = ((), (), s32[]{:S(2)}) async-start(), calls=%async_computation.3 | async-start | bytes 262144 | tf_op jit(solution)/shard_map/psum | solution.py:32
  336.4 12.2 %copy-start.1 = (f32[32,2048]{1,0:T(8,128)S(1)}, f32[32,2048]{1,0:T(8,128)}, u32[]{:S(2)}) copy-start(f32[32,2048]{1,0:T(8,128)} %all-reduce.10.cloned.1.call-done) | copy-start | bytes 786436
Sparse Core Ops, SparseCore 0:
  30.3 47.3 all-reduce.5
  89.9 175.8 all-reduce.7
  291.7 44.6 all-reduce.9
  348.7 175.9 all-reduce.11
where the time goes:
time: 543 us; the launch traced here: 542 us
  waiting for transfers between devices  444 us (82%)
  matrix products  42 us (8%)
  blocking collectives  32.9 us (6%)
  between operations  13.8 us (3%)
  other arithmetic  9.91 us (2%)
    psum x2, waiting for transfers between devices, per_device(): total = lax.psum(terms, 'conf')  351 us
    psum x2, waiting for transfers between devices, per_device(): denom = lax.psum(partial_den, 'state')  92.2 us
    dot_general x2, matrix products, per_device(): lax.dot_general(ratio, boltz, (((1,), (1,)), ((), ())), precision=lax.Pre...  24.3 us
    dot_general x2, matrix products, per_device(): partial_den = jnp.dot(scaled, boltz, precision=lax.Precision.HIGHEST)  17.8 us
    psum x2, blocking collectives, spread(): return lax.psum(block, axis)  16.9 us
  transfers between devices with their start and end apart: 4, of which 4 were waited for; matrix products, arithmetic and copies ran while one was open for 0% of the time, Pallas kernels for 0%

commit v1 on v0

v1 whole, which is shorter than its diff:
```python
import functools

import jax
import jax.numpy as jnp
from jax import lax
from jax.experimental import pallas as pl
from jax.experimental.pallas import tpu as pltpu
from jax.sharding import PartitionSpec as P

MESH = pl.DeviceIdType.MESH
ITERS = 2
B = 32
KS = 1024
NS = 2048
PIECES = 4
W = NS // PIECES
LOADS = 8
LW = NS // LOADS
GROUP = 8
RING = 8
F32 = jnp.float32
BF16 = jnp.bfloat16


def pack(column):
    lane = lax.broadcasted_iota(jnp.int32, (8, 128), 1) // 32
    out = jnp.broadcast_to(column[24:32], (8, 128))
    for j in (2, 1, 0):
        out = jnp.where(lane == j, jnp.broadcast_to(column[8 * j : 8 * j + 8], (8, 128)), out)
    return out


def unpack(tile):
    return jnp.concatenate([tile[:, 32 * j : 32 * j + 1] for j in range(4)], axis=0)


def split(x):
    high = x.astype(BF16)
    low = (x - high.astype(F32)).astype(BF16)
    return high, low


def kernel(
    e_hbm, samples_hbm, counts_hbm, initial_hbm, free_ref, lw_ref,
    e_buf, bh, bl, samples, counts, lifted, lhs, rhs, total, mine, log_samples,
    part1, part2, got1, got2, ext, ext_got, rows, rows_got, tot, tot_got, ring, ring_got, val, val_got,
    load_sem, small_sem, send_sem, recv_sem,
):
    c = lax.axis_index("conf")
    y = lax.axis_index("state")
    z, g = c // GROUP, c % GROUP
    peers = (y + 1 - 2 * (y % 2), 3 - y, (y + 2) % 4)

    loads = []
    small = [
        pltpu.make_async_copy(samples_hbm, samples, small_sem.at[0]),
        pltpu.make_async_copy(initial_hbm, lifted, small_sem.at[1]),
        pltpu.make_async_copy(counts_hbm, counts, small_sem.at[2]),
    ]
    small[0].start()
    small[1].start()
    for i in range(LOADS):
        copy = pltpu.make_async_copy(e_hbm.at[:, pl.ds(i * LW, LW)], e_buf.at[i], load_sem.at[i])
        copy.start()
        loads.append(copy)
    small[2].start()

    barrier = pltpu.get_barrier_semaphore()
    for peer in peers:
        pl.semaphore_signal(barrier, inc=1, device_id={"conf": c, "state": peer}, device_id_type=MESH)
    for o in range(1, GROUP):
        peer = z * GROUP + (g + o) % GROUP
        pl.semaphore_signal(barrier, inc=1, device_id={"conf": peer, "state": y}, device_id_type=MESH)
    for o in range(1, RING):
        peer = ((z + o) % RING) * GROUP + g
        pl.semaphore_signal(barrier, inc=1, device_id={"conf": peer, "state": y}, device_id_type=MESH)

    sent = []

    def send(src, dst, conf, state):
        n = len(sent)
        copy = pltpu.make_async_remote_copy(
            src_ref=src, dst_ref=dst, send_sem=send_sem.at[n], recv_sem=recv_sem.at[n],
            device_id={"conf": conf, "state": state}, device_id_type=MESH,
        )
        copy.start()
        sent.append(copy)
        return copy

    small[0].wait()
    small[1].wait()
    log_samples[...] = jnp.log(samples[...].astype(F32))
    for j in range(GROUP):
        cols = pl.ds(128 * j, 128)
        lifted[:, cols] = lifted[:, cols] + log_samples[j : j + 1, :]

    free_copies = None
    for it in range(ITERS):
        last = it == ITERS - 1
        top_me = jnp.max(lifted[...], axis=1, keepdims=True)
        mine[...] = jnp.broadcast_to(top_me, (B, 128))
        ext[it, 0] = pack(top_me)
        n_ext = 1
        if it > 0:
            first = jnp.where(y == 0, val_got[it - 1, 0, :, 0:1], jnp.zeros((B, 1), F32))
            ext[it, 1] = pack(first)
            n_ext = 2
        high, low = split(jnp.exp(lifted[...] - top_me))
        lhs[0:B, :] = high
        lhs[B : 2 * B, :] = low
        if it == 0:
            pl.semaphore_wait(barrier, 3 + GROUP - 1 + RING - 1)
        ext_copies = [send(ext.at[it, pl.ds(0, n_ext)], ext_got.at[it, k, pl.ds(0, n_ext)], c, peers[k]) for k in range(3)]

        row_copies = []
        phase1 = []
        for p in range(PIECES):
            if it == 0:
                for h in range(W // LW):
                    i = p * (W // LW) + h
                    loads[i].wait()

                    def low_energy(r, acc):
                        return jnp.minimum(acc, jnp.min(e_buf[i, pl.ds(r * 64, 64), :].reshape(8, 8, LW), axis=0))

                    least = lax.fori_loop(0, KS // 64, low_energy, jnp.full((8, LW), jnp.inf, F32), unroll=4)
                    shift = -jnp.min(least, axis=0, keepdims=True)
                    rows[p, 0:1, h * LW : (h + 1) * LW] = shift
                    rows[p, 1:2, h * LW : (h + 1) * LW] = jnp.where(y == 0, e_buf[i, 0:1, :], jnp.zeros((1, LW), F32))
                row_copies.append([send(rows.at[p], rows_got.at[k, p], c, peers[k]) for k in range(3)])
                for h in range(W // LW):
                    i = p * (W // LW) + h
                    shift = rows[p, 0:1, h * LW : (h + 1) * LW]

                    def boltz(r, carry):
                        at = pl.ds(r * 32, 32)
                        high, low = split(jnp.exp(-e_buf[i, at, :] - shift))
                        bh[p, at, h * LW : (h + 1) * LW] = high
                        bl[p, at, h * LW : (h + 1) * LW] = low
                        return carry

                    lax.fori_loop(0, KS // 32, boltz, 0, unroll=4)
            both = jnp.dot(lhs[...], bh[p], preferred_element_type=F32)
            rest = jnp.dot(lhs[0:B, :], bl[p], preferred_element_type=F32)
            part1[it, p] = both[0:B] + (both[B : 2 * B] + rest)
            phase1.append(send(part1.at[it, p], got1.at[it, p], c, peers[p % 2]))

        for copy in ext_copies:
            copy.wait_recv()
        tops = [mine[:, 0:1]] + [unpack(ext_got[it, k, 0]) for k in range(3)]
        pairs = [jnp.maximum(tops[0], tops[1]), jnp.maximum(tops[0], tops[2])]
        others = [jnp.maximum(tops[2], tops[3]), jnp.maximum(tops[1], tops[3])]
        top = jnp.maximum(pairs[0], others[0])
        own1 = [jnp.exp(tops[0] - pairs[k]) for k in range(2)]
        its1 = [jnp.exp(tops[1 + k] - pairs[k]) for k in range(2)]
        own2 = [jnp.exp(pairs[k] - top) for k in range(2)]
        its2 = [jnp.exp(others[k] - top) for k in range(2)]
        if it > 0:
            anchor = unpack(ext[it, 1])
            for k in range(3):
                anchor = anchor + unpack(ext_got[it, k, 1])
        phase2 = []
        for p in range(PIECES):
            k = p % 2
            a, b = own1[k], its1[k]
            if it == 0:
                for copy in row_copies[p]:
                    copy.wait_recv()
            m0, m1 = rows[p, 0:1, :], rows_got[k, p, 0:1, :]
            m = jnp.maximum(m0, m1)
            a, b = a * jnp.exp(m0 - m), b * jnp.exp(m1 - m)
            phase1[p].wait_recv()
            part2[it, p] = part1[it, p] * a + got1[it, p] * b
            phase2.append(send(part2.at[it, p], got2.at[it, p], c, peers[1 - k]))
        if it == 0:
            small[2].wait()
        first_total = jnp.zeros((B, 1), F32)
        for p in range(PIECES):
            k = p % 2
            a, b = own2[k], its2[k]
            ms = [rows[p, 0:1, :]] + [rows_got[j, p, 0:1, :] for j in range(3)]
            pair = jnp.maximum(ms[0], ms[1 + k])
            other = jnp.maximum(ms[2 - k], ms[3])
            m = jnp.maximum(pair, other)
            a, b = a * jnp.exp(pair - m), b * jnp.exp(other - m)
            phase2[p].wait_recv()
            denom = part2[it, p] * a + got2[it, p] * b
            ratio = counts[:, p * W : (p + 1) * W].astype(F32) / denom
            if last:
                lw_ref[:, p * W : (p + 1) * W] = jnp.log(denom) + (top - anchor)
                e0 = rows[p, 1:2, :] + rows_got[0, p, 1:2, :] + rows_got[1, p, 1:2, :] + rows_got[2, p, 1:2, :]
                first_total = first_total + jnp.sum(ratio * jnp.exp(-e0 - m), axis=1, keepdims=True)
            high, low = split(ratio * jnp.exp(ms[0] - m))
            rhs[0:B, :] = high
            rhs[B : 2 * B, :] = low
            dims = (((1,), (1,)), ((), ()))
            both = lax.dot_general(rhs[...], bh[p], dims, preferred_element_type=F32)
            rest = lax.dot_general(rhs[0:B, :], bl[p], dims, preferred_element_type=F32)
            terms = both[0:B] + (both[B : 2 * B] + rest)
            total[...] = terms if p == 0 else total[...] + terms

        height = B + 8 if last else B
        packed = pack(first_total) if last else None
        for j in range(GROUP):
            tot[it, j, 0:B, :] = total[:, 128 * j : 128 * (j + 1)]
            if last:
                tot[it, j, B : B + 8, :] = packed
        span = pl.ds(0, height)
        scatter = []
        for o in range(1, GROUP):
            to = (g + o) % GROUP
            scatter.append(send(tot.at[it, to, span], tot_got.at[it, o, span], z * GROUP + to, y))
        acc = tot[it, g, 0:height, :]
        for o in range(1, GROUP):
            scatter[o - 1].wait_recv()
            acc = acc + tot_got[it, o, 0:height, :]
        ring[it, 0:height, :] = acc
        ring_got[it, z, 0:height, :] = acc
        around = []
        for o in range(1, RING):
            around.append(send(ring.at[it, span], ring_got.at[it, z, span], ((z + o) % RING) * GROUP + g, y))
        for copy in around:
            copy.wait_recv()
        acc = ring_got[it, 0, 0:height, :]
        for k in range(1, RING):
            acc = acc + ring_got[it, k, 0:height, :]
        if last:
            value = jnp.log(unpack(acc[B : B + 8])) - jnp.log(acc[0:B])
        else:
            value = top - jnp.log(acc)
        val[it] = value
        val_got[it, g] = value
        gather = []
        for o in range(1, GROUP):
            to = (g + o) % GROUP
            gather.append(send(val.at[it], val_got.at[it, g], z * GROUP + to, y))
        for copy in gather:
            copy.wait_recv()
        for j in range(GROUP):
            cols = pl.ds(128 * j, 128)
            if last:
                free_ref[:, cols] = val_got[it, j]
            else:
                lifted[:, cols] = val_got[it, j] + log_samples[j : j + 1, :]
    for copy in sent:
        copy.wait_send()


def per_device(energies, samples, counts, initial):
    anywhere = pl.BlockSpec(memory_space=pl.ANY)
    inside = pl.BlockSpec(memory_space=pltpu.VMEM)
    copies = 3 * PIECES + ITERS * (3 + 2 * PIECES + 2 * (GROUP - 1) + RING - 1)
    vmem = pltpu.VMEM
    return pl.pallas_call(
        kernel,
        out_shape=(jax.ShapeDtypeStruct((B, KS), F32), jax.ShapeDtypeStruct((B, NS), F32)),
        in_specs=[anywhere] * 4,
        out_specs=(inside, inside),
        scratch_shapes=[
            vmem((LOADS, KS, LW), F32),
            vmem((PIECES, KS, W), BF16),
            vmem((PIECES, KS, W), BF16),
            vmem((GROUP, 128), jnp.int32),
            vmem((B, NS), jnp.int32),
            vmem((B, KS), F32),
            vmem((2 * B, KS), BF16),
            vmem((2 * B, W), BF16),
            vmem((B, KS), F32),
            vmem((B, 128), F32),
            vmem((GROUP, 128), F32),
            vmem((ITERS, PIECES, B, W), F32),
            vmem((ITERS, PIECES, B, W), F32),
            vmem((ITERS, PIECES, B, W), F32),
            vmem((ITERS, PIECES, B, W), F32),
            vmem((ITERS, 2, 8, 128), F32),
            vmem((ITERS, 3, 2, 8, 128), F32),
            vmem((PIECES, 2, W), F32),
            vmem((3, PIECES, 2, W), F32),
            vmem((ITERS, GROUP, B + 8, 128), F32),
            vmem((ITERS, GROUP, B + 8, 128), F32),
            vmem((ITERS, B + 8, 128), F32),
            vmem((ITERS, RING, B + 8, 128), F32),
            vmem((ITERS, B, 128), F32),
            vmem((ITERS, GROUP, B, 128), F32),
            pltpu.SemaphoreType.DMA((LOADS,)),
            pltpu.SemaphoreType.DMA((3,)),
            pltpu.SemaphoreType.DMA((copies,)),
            pltpu.SemaphoreType.DMA((copies,)),
        ],
        compiler_params=pltpu.CompilerParams(
            collective_id=0, has_side_effects=True, vmem_limit_bytes=56 * 2**20
        ),
    )(energies, samples.reshape(GROUP, 128), counts, initial)


def solution(mesh):
    in_specs = (P("state", "conf"), P("state"), P(None, "conf"), P(None, "state"))
    out_specs = (P(None, "state"), P(None, "conf"))
    return jax.shard_map(
        per_device, mesh=mesh, in_specs=in_specs, out_specs=out_specs, check_vma=False
    )
```

time: 543 us -> 70 us (0.13)
  waiting for transfers between devices: 444 us -> 0 us
  Pallas kernels: 0 us -> 66 us
  matrix products: 42 us -> 0 us
  blocking collectives: 32.9 us -> 0 us
  between operations: 13.8 us -> 0.64 us
  other arithmetic: 9.91 us -> 0 us
    psum x4 -> x0, waiting for transfers between devices: 444 us -> none  [the longest x2 351 us: per_device(): total = lax.psum(terms, 'conf')]
    pallas_call x0 -> x1, Pallas kernels: none -> 66 us  [per_device(): pl.pallas_call(kernel, out_shape=(jax.ShapeDtypeStruct((B, KS), F32), jax...]
    dot_general x4 -> x0, matrix products: 42 us -> none  [the longest x2 24.3 us: per_device(): lax.dot_general(ratio, boltz, (((1,), (1,)), ((), ())), precision=lax.Pre...]
    psum x2 -> x0, blocking collectives: 16.9 us -> none  [spread(): return lax.psum(block, axis)]
    pmax x2 -> x0, blocking collectives: 16 us -> none  [the longest x1 9.79 us: per_device(): shift = lax.pmax(jnp.max(-energies, axis=0), 'state')]
  transfers between devices with their start and end apart: 4 -> 0, of which waited for: 4 -> 0; matrix products, arithmetic and copies ran while one was open for 0% -> 0% of each run, Pallas kernels for 0% -> 0%
where the time goes in v1:
time: 70 us; the launch traced here: 69.9 us
  Pallas kernels  66 us (94%)
  local copies, waits for them, and re-layouts  3.24 us (5%)
    pallas_call x1, Pallas kernels, per_device(): pl.pallas_call(kernel, out_shape=(jax.ShapeDtypeStruct((B, KS), F32), jax...  66 us
    unnamed x2, local copies, waits for them, and re-layouts  3.24 us

profile of v1, /device:TPU:1, one launch (start us, length us, event | category | flops | bytes accessed | tf_op | source)
XLA Modules:
  0.0 69.9 jit_solution(3719285644725853737)
XLA Ops:
  0.6 66.0 %shard_map.59 = (f32[32,1024]{1,0:T(8,128)}, f32[32,2048]{1,0:T(8,128)}) custom-call(f32[1024,2048]{1,0:T(8,128)} %e_hbm.1, s32[8,128]{1,0:T(8,128)} %bitcast.1, s32[32,2048]{1,0:T(8,128)} %counts_hbm.1, f32[32,1024]{1,0:T(8,128)} %initial_hbm.1), custom_call_target="tpu_custom_call" | custom-call | tf_op jit(solution)/shard_map/pallas_call | solution.py:254
  66.7 1.6 %copy.8 = f32[32,1024]{1,0:T(8,128)} copy(f32[32,1024]{1,0:T(8,128)} %get-tuple-element.4) | data formatting | bytes 262144
  68.2 1.7 %copy.9 = f32[32,2048]{1,0:T(8,128)} copy(f32[32,2048]{1,0:T(8,128)} %get-tuple-element.5) | data formatting | bytes 524288

commit v2 on v1

v2 whole, which is shorter than its diff:
```python
import functools

import jax
import jax.numpy as jnp
from jax import lax
from jax.experimental import pallas as pl
from jax.experimental.pallas import tpu as pltpu
from jax.sharding import PartitionSpec as P

MESH = pl.DeviceIdType.MESH
ITERS = 2
B = 32
KS = 1024
NS = 2048
PIECES = 8
W = NS // PIECES
BATCH = 4
GROUP = 8
RING = 8
F32 = jnp.float32
BF16 = jnp.bfloat16


def diagonal(offset):
    return lax.broadcasted_iota(jnp.int32, (B, 128), 1) == lax.broadcasted_iota(jnp.int32, (B, 128), 0) + offset


def to_row(column, offset=0):
    return jnp.sum(jnp.where(diagonal(offset), column, 0.0), axis=0, keepdims=True)


def to_column(row, offset=0):
    return jnp.sum(jnp.where(diagonal(offset), row, 0.0), axis=1, keepdims=True)


def split(x):
    high = x.astype(BF16)
    low = (x - high.astype(F32)).astype(BF16)
    return high, low


def kernel(
    e_hbm, samples_hbm, counts_hbm, initial_hbm, free_ref, lw_ref,
    e_buf, bh, bl, samples, counts, lifted, lhs, rhs, mine, log_samples,
    part1, part2, got1, got2, ext, ext_got, rows, rows_got, tot, tot_got, ring, ring_got, val, val_got,
    load_sem, small_sem, send_sem, recv_sem,
):
    c = lax.axis_index("conf")
    y = lax.axis_index("state")
    z, g = c // GROUP, c % GROUP
    peers = (y + 1 - 2 * (y % 2), 3 - y, (y + 2) % 4)

    barrier = pltpu.get_barrier_semaphore()
    for peer in peers:
        pl.semaphore_signal(barrier, inc=1, device_id={"conf": c, "state": peer}, device_id_type=MESH)
    for o in range(1, GROUP):
        peer = z * GROUP + (g + o) % GROUP
        pl.semaphore_signal(barrier, inc=1, device_id={"conf": peer, "state": y}, device_id_type=MESH)
    for o in range(1, RING):
        peer = ((z + o) % RING) * GROUP + g
        pl.semaphore_signal(barrier, inc=1, device_id={"conf": peer, "state": y}, device_id_type=MESH)

    loads = []
    small = [
        pltpu.make_async_copy(samples_hbm, samples, small_sem.at[0]),
        pltpu.make_async_copy(initial_hbm, lifted, small_sem.at[1]),
        pltpu.make_async_copy(counts_hbm, counts, small_sem.at[2]),
    ]
    small[0].start()
    small[1].start()
    for i in range(PIECES):
        copy = pltpu.make_async_copy(e_hbm.at[:, pl.ds(i * W, W)], e_buf.at[i], load_sem.at[i])
        copy.start()
        loads.append(copy)
    small[2].start()

    sent = []

    def send(src, dst, conf, state):
        n = len(sent)
        copy = pltpu.make_async_remote_copy(
            src_ref=src, dst_ref=dst, send_sem=send_sem.at[n], recv_sem=recv_sem.at[n],
            device_id={"conf": conf, "state": state}, device_id_type=MESH,
        )
        copy.start()
        sent.append(copy)
        return copy

    drained = [0]

    def drain():
        for copy in sent[drained[0] :]:
            copy.wait_send()
        drained[0] = len(sent)

    small[0].wait()
    small[1].wait()
    log_samples[...] = jnp.log(samples[...].astype(F32))
    for j in range(GROUP):
        cols = pl.ds(128 * j, 128)
        lifted[:, cols] = lifted[:, cols] + log_samples[j : j + 1, :]

    free_copies = None
    for it in range(ITERS):
        last = it == ITERS - 1
        top_me = jnp.max(lifted[...], axis=1, keepdims=True)
        mine[...] = jnp.broadcast_to(top_me, (B, 128))
        line = to_row(top_me)
        if it > 0:
            line = line + to_row(jnp.where(y == 0, val_got[it - 1, 0, :, 0:1], jnp.zeros((B, 1), F32)), B)
        ext[it] = line
        high, low = split(jnp.exp(lifted[...] - top_me))
        lhs[0:B, :] = high
        lhs[B : 2 * B, :] = low
        row_copies = []
        phase1 = []
        if it == 0:
            pl.semaphore_wait(barrier, 3 + GROUP - 1 + RING - 1)
        ext_copies = [send(ext.at[it], ext_got.at[it, k], c, peers[k]) for k in (2, 0, 1)]
        for p in range(PIECES):
            if it == 0:
                loads[p].wait()

                def low_energy(r, acc):
                    return jnp.minimum(acc, jnp.min(e_buf[p, pl.ds(r * 64, 64), :].reshape(8, 8, W), axis=0))

                least = lax.fori_loop(0, KS // 64, low_energy, jnp.full((8, W), jnp.inf, F32), unroll=4)
                shift = -jnp.min(least, axis=0, keepdims=True)
                q, cols = p // BATCH, slice(p % BATCH * W, (p % BATCH + 1) * W)
                rows[q, 0:1, cols] = shift
                rows[q, 1:2, cols] = jnp.where(y == 0, e_buf[p, 0:1, :], jnp.zeros((1, W), F32))
                if p % BATCH == BATCH - 1:
                    row_copies.append([send(rows.at[q], rows_got.at[k, q], c, peers[k]) for k in (2, 0, 1)])

                def boltz(r, carry):
                    at = pl.ds(r * 32, 32)
                    high, low = split(jnp.exp(-e_buf[p, at, :] - shift))
                    bh[p, at, :] = high
                    bl[p, at, :] = low
                    return carry

                lax.fori_loop(0, KS // 32, boltz, 0, unroll=4)
            both = jnp.dot(lhs[...], bh[p], preferred_element_type=F32)
            rest = jnp.dot(lhs[0:B, :], bl[p], preferred_element_type=F32)
            part1[it, p] = both[0:B] + (both[B : 2 * B] + rest)
            phase1.append(send(part1.at[it, p], got1.at[it, p], c, peers[p % 2]))

        for copy in ext_copies:
            copy.wait_recv()
        tops = [mine[:, 0:1]] + [to_column(ext_got[it, k]) for k in range(3)]
        pairs = [jnp.maximum(tops[0], tops[1]), jnp.maximum(tops[0], tops[2])]
        others = [jnp.maximum(tops[2], tops[3]), jnp.maximum(tops[1], tops[3])]
        top = jnp.maximum(pairs[0], others[0])
        own1 = [jnp.exp(tops[0] - pairs[k]) for k in range(2)]
        its1 = [jnp.exp(tops[1 + k] - pairs[k]) for k in range(2)]
        own2 = [jnp.exp(pairs[k] - top) for k in range(2)]
        its2 = [jnp.exp(others[k] - top) for k in range(2)]
        if it > 0:
            line = ext[it] + (ext_got[it, 0] + (ext_got[it, 1] + ext_got[it, 2]))
            anchor = to_column(line, B)
        phase2 = []
        for p in range(PIECES):
            k = p % 2
            a, b = own1[k], its1[k]
            q, cols = p // BATCH, slice(p % BATCH * W, (p % BATCH + 1) * W)
            if it == 0 and p % BATCH == 0:
                for copy in row_copies[q]:
                    copy.wait_recv()
            m0, m1 = rows[q, 0:1, cols], rows_got[k, q, 0:1, cols]
            m = jnp.maximum(m0, m1)
            a, b = a * jnp.exp(m0 - m), b * jnp.exp(m1 - m)
            phase1[p].wait_recv()
            part2[it, p] = part1[it, p] * a + got1[it, p] * b
            phase2.append(send(part2.at[it, p], got2.at[it, p], c, peers[1 - k]))
        if it == 0:
            small[2].wait()
        first_total = jnp.zeros((B, 128), F32)
        for p in range(PIECES):
            k = p % 2
            a, b = own2[k], its2[k]
            q, cols = p // BATCH, slice(p % BATCH * W, (p % BATCH + 1) * W)
            ms = [rows[q, 0:1, cols]] + [rows_got[j, q, 0:1, cols] for j in range(3)]
            pair = jnp.maximum(ms[0], ms[1 + k])
            other = jnp.maximum(ms[2 - k], ms[3])
            m = jnp.maximum(pair, other)
            a, b = a * jnp.exp(pair - m), b * jnp.exp(other - m)
            if last:
                e0 = rows[q, 1:2, cols] + rows_got[0, q, 1:2, cols] + rows_got[1, q, 1:2, cols] + rows_got[2, q, 1:2, cols]
                first_boltz = jnp.exp(-e0 - m)
            phase2[p].wait_recv()
            denom = part2[it, p] * a + got2[it, p] * b
            ratio = counts[:, p * W : (p + 1) * W].astype(F32) / denom
            if last:
                lw_ref[:, p * W : (p + 1) * W] = denom
                first_terms = ratio * first_boltz
                first_total = first_total + (first_terms[:, :128] + first_terms[:, 128:])
            high, low = split(ratio * jnp.exp(ms[0] - m))
            rhs[0:B, :] = high
            rhs[B : 2 * B, :] = low
            dims = (((1,), (1,)), ((), ()))
            if p < PIECES - 1:
                both = lax.dot_general(rhs[...], bh[p], dims, preferred_element_type=F32)
                rest = lax.dot_general(rhs[0:B, :], bl[p], dims, preferred_element_type=F32)
                terms = both[0:B] + (both[B : 2 * B] + rest)
                for j in range(GROUP):
                    part = terms[:, 128 * j : 128 * (j + 1)]
                    tot[it, j, 0:B, :] = part if p == 0 else tot[it, j, 0:B, :] + part

        height = B + 1 if last else B
        span = pl.ds(0, height)
        if last:
            first_line = to_row(jnp.sum(first_total, axis=1, keepdims=True))
            for j in range(GROUP):
                tot[it, j, B : B + 1, :] = first_line
        scatter = []
        p = PIECES - 1
        for ox in (2, 1, 3, 0):
            x = (g // 2 + ox) % (GROUP // 2)
            at = pl.ds(pl.multiple_of(x * 256, 256), 256)
            both = lax.dot_general(rhs[...], bh[p, at, :], dims, preferred_element_type=F32)
            rest = lax.dot_general(rhs[0:B, :], bl[p, at, :], dims, preferred_element_type=F32)
            terms = both[0:B] + (both[B : 2 * B] + rest)
            for core in range(2):
                j = 2 * x + core
                tot[it, j, 0:B, :] = tot[it, j, 0:B, :] + terms[:, 128 * core : 128 * (core + 1)]
            for oc in (0, 1):
                if ox == 0 and oc == 0:
                    continue
                slot = 2 * ox + oc
                to = 2 * x + (g + oc) % 2
                scatter.append((slot, send(tot.at[it, to, span], tot_got.at[it, slot, span], z * GROUP + to, y)))
        if it == 0:
            drain()
        acc = tot[it, g, 0:height, :]
        for slot, copy in scatter[::-1]:
            copy.wait_recv()
            acc = acc + tot_got[it, slot, 0:height, :]
        ring[it, 0:height, :] = acc
        around = []
        for o in (4, 3, 5, 2, 6, 1, 7):
            around.append(send(ring.at[it, span], ring_got.at[it, z, span], ((z + o) % RING) * GROUP + g, y))
        ring_got[it, z, 0:height, :] = acc
        drain()
        if last:
            for p in range(PIECES):
                cols = pl.ds(p * W, W)
                lw_ref[:, cols] = jnp.log(lw_ref[:, cols]) + (top - anchor)
        for copy in around:
            copy.wait_recv()
        acc = ring_got[it, 0, 0:height, :]
        for k in range(1, RING):
            acc = acc + ring_got[it, k, 0:height, :]
        if last:
            value = jnp.log(to_column(acc[B : B + 1])) - jnp.log(acc[0:B])
        else:
            value = top - jnp.log(acc)
        val[it] = value
        gather = []
        for ox, oc in ((2, 0), (2, 1), (1, 0), (1, 1), (3, 0), (3, 1), (0, 1)):
            to = 2 * ((g // 2 + ox) % (GROUP // 2)) + (g + oc) % 2
            gather.append(send(val.at[it], val_got.at[it, g], z * GROUP + to, y))
        val_got[it, g] = value
        for copy in gather:
            copy.wait_recv()
        for j in range(GROUP):
            cols = pl.ds(128 * j, 128)
            if last:
                free_ref[:, cols] = val_got[it, j]
            else:
                lifted[:, cols] = val_got[it, j] + log_samples[j : j + 1, :]
    drain()


def finish(free_in, lw_in, free_out, lw_out):
    free_out[...] = free_in[...]
    lw_out[...] = lw_in[...]


def per_device(energies, samples, counts, initial):
    outside = pl.BlockSpec(memory_space=pl.ANY)
    inside = pl.BlockSpec(memory_space=pltpu.VMEM)
    copies = 3 * PIECES // BATCH + ITERS * (3 + 2 * PIECES + 2 * (GROUP - 1) + RING - 1)
    vmem = pltpu.VMEM
    free, log_weight = pl.pallas_call(
        kernel,
        out_shape=tuple(jax.ShapeDtypeStruct((B, n), F32) for n in (KS, NS)),
        in_specs=[outside] * 4,
        out_specs=(inside,) * 2,
        scratch_shapes=[
            vmem((PIECES, KS, W), F32),
            vmem((PIECES, KS, W), BF16),
            vmem((PIECES, KS, W), BF16),
            vmem((GROUP, 128), jnp.int32),
            vmem((B, NS), jnp.int32),
            vmem((B, KS), F32),
            vmem((2 * B, KS), BF16),
            vmem((2 * B, W), BF16),
            vmem((B, 128), F32),
            vmem((GROUP, 128), F32),
            vmem((ITERS, PIECES, B, W), F32),
            vmem((ITERS, PIECES, B, W), F32),
            vmem((ITERS, PIECES, B, W), F32),
            vmem((ITERS, PIECES, B, W), F32),
            vmem((ITERS, 1, 128), F32),
            vmem((ITERS, 3, 1, 128), F32),
            vmem((PIECES // BATCH, 2, BATCH * W), F32),
            vmem((3, PIECES // BATCH, 2, BATCH * W), F32),
            vmem((ITERS, GROUP, B + 8, 128), F32),
            vmem((ITERS, GROUP, B + 8, 128), F32),
            vmem((ITERS, B + 8, 128), F32),
            vmem((ITERS, RING, B + 8, 128), F32),
            vmem((ITERS, B, 128), F32),
            vmem((ITERS, GROUP, B, 128), F32),
            pltpu.SemaphoreType.DMA((PIECES,)),
            pltpu.SemaphoreType.DMA((3,)),
            pltpu.SemaphoreType.DMA((copies,)),
            pltpu.SemaphoreType.DMA((copies,)),
        ],
        compiler_params=pltpu.CompilerParams(
            collective_id=0, has_side_effects=True, vmem_limit_bytes=56 * 2**20
        ),
    )(energies, samples.reshape(GROUP, 128), counts, initial)
    return pl.pallas_call(
        finish,
        out_shape=(jax.ShapeDtypeStruct((B, KS), F32), jax.ShapeDtypeStruct((B, NS), F32)),
        in_specs=[inside] * 2,
        out_specs=(inside,) * 2,
    )(free, log_weight)


def solution(mesh):
    in_specs = (P("state", "conf"), P("state"), P(None, "conf"), P(None, "state"))
    out_specs = (P(None, "state"), P(None, "conf"))
    return jax.shard_map(
        per_device, mesh=mesh, in_specs=in_specs, out_specs=out_specs, check_vma=False
    )
```

time: 70 us -> 67.8 us (0.969)
  local copies, waits for them, and re-layouts: 3.24 us -> 0 us
  Pallas kernels: 66 us -> 67 us
    unnamed x2 -> x0, local copies, waits for them, and re-layouts: 3.24 us -> none
    pallas_call x1 -> x2, Pallas kernels: 66 us -> 67 us  [the longest x1 65.2 us: per_device(): pl.pallas_call(kernel, out_shape=tuple((jax.ShapeDtypeStruct((B, n), F32)...]
where the time goes in v2:
time: 67.8 us; the launch traced here: 67.7 us
  Pallas kernels  67 us (99%)
    pallas_call x1, Pallas kernels, per_device(): pl.pallas_call(kernel, out_shape=tuple((jax.ShapeDtypeStruct((B, n), F32)...  65.2 us
    pallas_call x1, Pallas kernels, per_device(): pl.pallas_call(finish, out_shape=(jax.ShapeDtypeStruct((B, KS), F32), jax...  1.78 us

profile of v2, /device:TPU:1, one launch (start us, length us, event | category | flops | bytes accessed | tf_op | source)
XLA Modules:
  0.0 67.7 jit_solution(4123660217636150024)
XLA Ops:
  0.6 65.2 %shard_map.59 = (f32[32,1024]{1,0:T(8,128)}, f32[32,2048]{1,0:T(8,128)}) custom-call(f32[1024,2048]{1,0:T(8,128)} %e_hbm.1, s32[8,128]{1,0:T(8,128)} %bitcast.1, s32[32,2048]{1,0:T(8,128)} %counts_hbm.1, f32[32,1024]{1,0:T(8,128)} %initial_hbm.1), custom_call_target="tpu_custom_call" | custom-call | tf_op jit(solution)/shard_map/pallas_call | solution.py:284
  65.9 1.8 %shard_map.60 = (f32[32,1024]{1,0:T(8,128)}, f32[32,2048]{1,0:T(8,128)}) custom-call(f32[32,1024]{1,0:T(8,128)} %get-tuple-element.4.free_in, f32[32,2048]{1,0:T(8,128)} %get-tuple-element.5.lw_in), custom_call_target="tpu_custom_call" | custom-call | tf_op jit(solution)/shard_map/pallas_call | solution.py:323

commit v3 on v2

v3 whole, which is shorter than its diff:
```python
import functools

import jax
import jax.numpy as jnp
from jax import lax
from jax.experimental import pallas as pl
from jax.experimental.pallas import tpu as pltpu
from jax.sharding import PartitionSpec as P

MESH = pl.DeviceIdType.MESH
ITERS = 2
B = 32
KS = 1024
NS = 2048
PIECES = 8
W = NS // PIECES
PAIRS = PIECES // 2
DEEP = 256
GROUP = 8
RING = 8
F32 = jnp.float32
BF16 = jnp.bfloat16


def diagonal(offset):
    return lax.broadcasted_iota(jnp.int32, (B, 128), 1) == lax.broadcasted_iota(jnp.int32, (B, 128), 0) + offset


def to_row(column, offset=0):
    return jnp.sum(jnp.where(diagonal(offset), column, 0.0), axis=0, keepdims=True)


def to_column(row, offset=0):
    return jnp.sum(jnp.where(diagonal(offset), row, 0.0), axis=1, keepdims=True)


def split(x):
    high = x.astype(BF16)
    low = (x - high.astype(F32)).astype(BF16)
    return high, low


def kernel(
    e_hbm, samples_hbm, counts_hbm, initial_hbm, free_ref, lw_ref,
    e_buf, bh, bl, samples, counts, lifted, lhs, rhs, mine, log_samples,
    part1, part2, got1, got2, ext, ext_got, rows, rows_got, tot, tot_got, ring, ring_got, val, val_got,
    load_sem, small_sem, send_sem, recv_sem,
):
    c = lax.axis_index("conf")
    y = lax.axis_index("state")
    z, g = c // GROUP, c % GROUP
    peers = (y + 1 - 2 * (y % 2), 3 - y, (y + 2) % 4)

    barrier = pltpu.get_barrier_semaphore()
    for peer in peers:
        pl.semaphore_signal(barrier, inc=1, device_id={"conf": c, "state": peer}, device_id_type=MESH)
    for o in range(1, GROUP):
        peer = z * GROUP + (g + o) % GROUP
        pl.semaphore_signal(barrier, inc=1, device_id={"conf": peer, "state": y}, device_id_type=MESH)
    for o in range(1, RING):
        peer = ((z + o) % RING) * GROUP + g
        pl.semaphore_signal(barrier, inc=1, device_id={"conf": peer, "state": y}, device_id_type=MESH)

    small = [
        pltpu.make_async_copy(samples_hbm, samples, small_sem.at[0]),
        pltpu.make_async_copy(initial_hbm, lifted, small_sem.at[1]),
        pltpu.make_async_copy(counts_hbm, counts, small_sem.at[2]),
    ]
    small[0].start()
    small[1].start()
    loads = [pltpu.make_async_copy(e_hbm.at[:, pl.ds(p * W, W)], e_buf.at[p], load_sem.at[p]) for p in range(PIECES)]
    for copy in loads:
        copy.start()
    small[2].start()

    def remote(src, dst, conf, state, n):
        return pltpu.make_async_remote_copy(
            src_ref=src, dst_ref=dst, send_sem=send_sem.at[n], recv_sem=recv_sem.at[n],
            device_id={"conf": conf, "state": state}, device_id_type=MESH,
        )

    used = [0]

    def take(n):
        used[0] += n
        return used[0] - n

    undrained = []

    def send(src, dst, conf, state):
        copy = remote(src, dst, conf, state, take(1))
        copy.start()
        undrained.append(copy.wait_send)
        return copy

    def drain():
        for wait in undrained:
            wait()
        undrained.clear()

    def row_copies(t, k):
        return remote(rows.at[t], rows_got.at[k, t], c, peers[k], row_base + 3 * t + k)

    def wait_rows():
        @pl.loop(0, PAIRS)
        def _(t):
            for k in range(3):
                row_copies(t, k).wait_send()

    row_base = take(3 * PAIRS)

    small[0].wait()
    small[1].wait()
    log_samples[...] = jnp.log(samples[...].astype(F32))
    for j in range(GROUP):
        cols = pl.ds(128 * j, 128)
        lifted[:, cols] = lifted[:, cols] + log_samples[j : j + 1, :]

    for it in range(ITERS):
        last = it == ITERS - 1
        top_me = jnp.max(lifted[...], axis=1, keepdims=True)
        mine[...] = jnp.broadcast_to(top_me, (B, 128))
        high, low = split(jnp.exp(lifted[...] - top_me))
        lhs[0:B, :] = high
        lhs[B : 2 * B, :] = low
        line = to_row(top_me)
        if it > 0:
            line = line + to_row(jnp.where(y == 0, val_got[it - 1, 0, :, 0:1], jnp.zeros((B, 1), F32)), B)
        ext[it] = line
        if it == 0:
            pl.semaphore_wait(barrier, 3 + GROUP - 1 + RING - 1)
        ext_copies = [send(ext.at[it], ext_got.at[it, k], c, peers[k]) for k in (2, 0, 1)]
        base1, base2 = take(PIECES), take(PIECES)

        def copy1(p, k):
            return remote(part1.at[it, p], got1.at[it, p], c, peers[k], base1 + p)

        def copy2(p, k):
            return remote(part2.at[it, p], got2.at[it, p], c, peers[1 - k], base2 + p)

        def wait_parts():
            @pl.loop(0, PAIRS)
            def _(t):
                for k in range(2):
                    copy1(2 * t + k, k).wait_send()
                    copy2(2 * t + k, k).wait_send()

        @pl.loop(0, PAIRS)
        def _(t):
            leasts = []
            if it == 0:
                for k in range(2):
                    p = 2 * t + k
                    pltpu.make_async_copy(e_hbm.at[:, pl.ds(0, W)], e_buf.at[p], load_sem.at[p]).wait()

                    def low_energy(r, acc):
                        return jnp.minimum(acc, jnp.min(e_buf[p, pl.ds(r * 64, 64), :].reshape(8, 8, W), axis=0))

                    least = lax.fori_loop(0, KS // 64, low_energy, jnp.full((8, W), jnp.inf, F32), unroll=16)
                    least = jnp.min(least, axis=0, keepdims=True)
                    cols = slice(k * W, (k + 1) * W)
                    rows[t, 0:1, cols] = -least
                    rows[t, 1:2, cols] = jnp.where(y == 0, e_buf[p, 0:1, :], jnp.zeros((1, W), F32))
                    leasts.append(least)
                for k in (2, 0, 1):
                    row_copies(t, k).start()
            for k in range(2):
                p = 2 * t + k
                if it == 0:
                    acc = jnp.zeros((B, W), F32)
                    for d in range(KS // DEEP):
                        for r in range(d * DEEP, (d + 1) * DEEP, 32):
                            high, low = split(jnp.exp(leasts[k] - e_buf[p, r : r + 32, :]))
                            bh[p, r : r + 32, :] = high
                            bl[p, r : r + 32, :] = low
                        at = slice(d * DEEP, (d + 1) * DEEP)
                        both = jnp.dot(lhs[:, at], bh[p, at, :], preferred_element_type=F32)
                        rest = jnp.dot(lhs[0:B, at], bl[p, at, :], preferred_element_type=F32)
                        acc = acc + (both[0:B] + (both[B : 2 * B] + rest))
                    part1[it, p] = acc
                else:
                    both = jnp.dot(lhs[...], bh[p], preferred_element_type=F32)
                    rest = jnp.dot(lhs[0:B, :], bl[p], preferred_element_type=F32)
                    part1[it, p] = both[0:B] + (both[B : 2 * B] + rest)
                copy1(p, k).start()

        for copy in ext_copies:
            copy.wait_recv()
        tops = [mine[:, 0:1]] + [to_column(ext_got[it, k]) for k in range(3)]
        pairs = [jnp.maximum(tops[0], tops[1]), jnp.maximum(tops[0], tops[2])]
        others = [jnp.maximum(tops[2], tops[3]), jnp.maximum(tops[1], tops[3])]
        top = jnp.maximum(pairs[0], others[0])
        own1 = [jnp.exp(tops[0] - pairs[k]) for k in range(2)]
        its1 = [jnp.exp(tops[1 + k] - pairs[k]) for k in range(2)]
        own2 = [jnp.exp(pairs[k] - top) for k in range(2)]
        its2 = [jnp.exp(others[k] - top) for k in range(2)]
        if it > 0:
            line = ext[it] + (ext_got[it, 0] + (ext_got[it, 1] + ext_got[it, 2]))
            anchor = to_column(line, B)

        @pl.loop(0, PAIRS)
        def _(t):
            if it == 0:
                for k in range(3):
                    row_copies(t, k).wait_recv()
            for k in range(2):
                p = 2 * t + k
                cols = slice(k * W, (k + 1) * W)
                m0, m1 = rows[t, 0:1, cols], rows_got[k, t, 0:1, cols]
                m = jnp.maximum(m0, m1)
                a, b = own1[k] * jnp.exp(m0 - m), its1[k] * jnp.exp(m1 - m)
                copy1(p, k).wait_recv()
                part2[it, p] = part1[it, p] * a + got1[it, p] * b
                copy2(p, k).start()

        tot[it] = jnp.zeros((GROUP, B + 8, 128), F32)
        if it == 0:
            small[2].wait()
        dims = (((1,), (1,)), ((), ()))

        def ratios(t, k, first_total):
            p = 2 * t + k
            cols = slice(k * W, (k + 1) * W)
            ms = [rows[t, 0:1, cols]] + [rows_got[j, t, 0:1, cols] for j in range(3)]
            pair = jnp.maximum(ms[0], ms[1 + k])
            other = jnp.maximum(ms[2 - k], ms[3])
            m = jnp.maximum(pair, other)
            a, b = own2[k] * jnp.exp(pair - m), its2[k] * jnp.exp(other - m)
            own_scale = jnp.exp(ms[0] - m)
            whole = pl.ds(pl.multiple_of(p * W, W), W)
            weight = counts[:, whole].astype(F32)
            if last:
                e0 = rows[t, 1:2, cols] + rows_got[0, t, 1:2, cols] + rows_got[1, t, 1:2, cols] + rows_got[2, t, 1:2, cols]
                first_boltz = jnp.exp(-e0 - m)
            copy2(p, k).wait_recv()
            denom = part2[it, p] * a + got2[it, p] * b
            ratio = weight / denom
            high, low = split(ratio * own_scale)
            rhs[k, 0:B, :] = high
            rhs[k, B : 2 * B, :] = low
            if last:
                lw_ref[:, whole] = denom
                first_terms = ratio * first_boltz
                first_total = first_total + (first_terms[:, :128] + first_terms[:, 128:])
            return first_total

        def terms(p, k, x):
            at = pl.ds(pl.multiple_of(x * 256, 256), 256)
            both = lax.dot_general(rhs[k], bh[p, at, :], dims, preferred_element_type=F32)
            rest = lax.dot_general(rhs[k, 0:B, :], bl[p, at, :], dims, preferred_element_type=F32)
            made = both[0:B] + (both[B : 2 * B] + rest)
            for core in range(2):
                j = 2 * x + core
                tot[it, j, 0:B, :] = tot[it, j, 0:B, :] + made[:, 128 * core : 128 * (core + 1)]

        def both_pieces(t, first_total):
            for k in range(2):
                first_total = ratios(t, k, first_total)
                for x in range(GROUP // 2):
                    terms(2 * t + k, k, x)
            return first_total

        first_total = lax.fori_loop(0, PAIRS - 1, both_pieces, jnp.zeros((B, 128), F32))
        first_total = ratios(PAIRS - 1, 0, first_total)
        for x in range(GROUP // 2):
            terms(PIECES - 2, 0, x)
        first_total = ratios(PAIRS - 1, 1, first_total)

        height = B + 1 if last else B
        span = pl.ds(0, height)
        if last:
            first_line = to_row(jnp.sum(first_total, axis=1, keepdims=True))
            for j in range(GROUP):
                tot[it, j, B : B + 1, :] = first_line
        scatter = []
        for ox in (2, 1, 3, 0):
            x = (g // 2 + ox) % (GROUP // 2)
            terms(PIECES - 1, 1, x)
            for oc in (0, 1):
                if ox == 0 and oc == 0:
                    continue
                slot = 2 * ox + oc
                to = 2 * x + (g + oc) % 2
                scatter.append((slot, send(tot.at[it, to, span], tot_got.at[it, slot, span], z * GROUP + to, y)))
        if it == 0:
            wait_rows()
        wait_parts()
        acc = tot[it, g, 0:height, :]
        for slot, copy in scatter[::-1]:
            copy.wait_recv()
            acc = acc + tot_got[it, slot, 0:height, :]
        ring[it, 0:height, :] = acc
        around = []
        for o in (4, 3, 5, 2, 6, 1, 7):
            around.append(send(ring.at[it, span], ring_got.at[it, z, span], ((z + o) % RING) * GROUP + g, y))
        ring_got[it, z, 0:height, :] = acc
        drain()
        if last:

            @pl.loop(0, PIECES)
            def _(p):
                whole = pl.ds(pl.multiple_of(p * W, W), W)
                lw_ref[:, whole] = jnp.log(lw_ref[:, whole]) + (top - anchor)

        for copy in around:
            copy.wait_recv()
        acc = ring_got[it, 0, 0:height, :]
        for k in range(1, RING):
            acc = acc + ring_got[it, k, 0:height, :]
        if last:
            value = jnp.log(to_column(acc[B : B + 1])) - jnp.log(acc[0:B])
        else:
            value = top - jnp.log(acc)
        val[it] = value
        gather = []
        for ox, oc in ((2, 0), (2, 1), (1, 0), (1, 1), (3, 0), (3, 1), (0, 1)):
            to = 2 * ((g // 2 + ox) % (GROUP // 2)) + (g + oc) % 2
            gather.append(send(val.at[it], val_got.at[it, g], z * GROUP + to, y))
        val_got[it, g] = value
        for copy in gather:
            copy.wait_recv()
        for j in range(GROUP):
            cols = pl.ds(128 * j, 128)
            if last:
                free_ref[:, cols] = val_got[it, j]
            else:
                lifted[:, cols] = val_got[it, j] + log_samples[j : j + 1, :]
    drain()


def finish(free_in, lw_in, free_out, lw_out):
    free_out[...] = free_in[...]
    lw_out[...] = lw_in[...]


def per_device(energies, samples, counts, initial):
    outside = pl.BlockSpec(memory_space=pl.ANY)
    inside = pl.BlockSpec(memory_space=pltpu.VMEM)
    copies = 3 * PAIRS + ITERS * (3 + 2 * PIECES + 2 * (GROUP - 1) + RING - 1)
    vmem = pltpu.VMEM
    free, log_weight = pl.pallas_call(
        kernel,
        out_shape=tuple(jax.ShapeDtypeStruct((B, n), F32) for n in (KS, NS)),
        in_specs=[outside] * 4,
        out_specs=(inside,) * 2,
        scratch_shapes=[
            vmem((PIECES, KS, W), F32),
            vmem((PIECES, KS, W), BF16),
            vmem((PIECES, KS, W), BF16),
            vmem((GROUP, 128), jnp.int32),
            vmem((B, NS), jnp.int32),
            vmem((B, KS), F32),
            vmem((2 * B, KS), BF16),
            vmem((2, 2 * B, W), BF16),
            vmem((B, 128), F32),
            vmem((GROUP, 128), F32),
            vmem((ITERS, PIECES, B, W), F32),
            vmem((ITERS, PIECES, B, W), F32),
            vmem((ITERS, PIECES, B, W), F32),
            vmem((ITERS, PIECES, B, W), F32),
            vmem((ITERS, 1, 128), F32),
            vmem((ITERS, 3, 1, 128), F32),
            vmem((PAIRS, 2, 2 * W), F32),
            vmem((3, PAIRS, 2, 2 * W), F32),
            vmem((ITERS, GROUP, B + 8, 128), F32),
            vmem((ITERS, GROUP, B + 8, 128), F32),
            vmem((ITERS, B + 8, 128), F32),
            vmem((ITERS, RING, B + 8, 128), F32),
            vmem((ITERS, B, 128), F32),
            vmem((ITERS, GROUP, B, 128), F32),
            pltpu.SemaphoreType.DMA((PIECES,)),
            pltpu.SemaphoreType.DMA((3,)),
            pltpu.SemaphoreType.DMA((copies,)),
            pltpu.SemaphoreType.DMA((copies,)),
        ],
        compiler_params=pltpu.CompilerParams(
            collective_id=0, has_side_effects=True, vmem_limit_bytes=56 * 2**20
        ),
    )(energies, samples.reshape(GROUP, 128), counts, initial)
    return pl.pallas_call(
        finish,
        out_shape=(jax.ShapeDtypeStruct((B, KS), F32), jax.ShapeDtypeStruct((B, NS), F32)),
        in_specs=[inside] * 2,
        out_specs=(inside,) * 2,
    )(free, log_weight)


def solution(mesh):
    in_specs = (P("state", "conf"), P("state"), P(None, "conf"), P(None, "state"))
    out_specs = (P(None, "state"), P(None, "conf"))
    return jax.shard_map(
        per_device, mesh=mesh, in_specs=in_specs, out_specs=out_specs, check_vma=False
    )
```

time: 67.8 us -> 64.8 us (0.956)
  Pallas kernels: 67 us -> 64.1 us
    pallas_call x1, Pallas kernels: 65.2 us -> 62.3 us  [per_device(): pl.pallas_call(kernel, out_shape=tuple((jax.ShapeDtypeStruct((B, n), F32)...]
where the time goes in v3:
time: 64.8 us; the launch traced here: 64.7 us
  Pallas kernels  64.1 us (99%)
    pallas_call x1, Pallas kernels, per_device(): pl.pallas_call(kernel, out_shape=tuple((jax.ShapeDtypeStruct((B, n), F32)...  62.3 us
    pallas_call x1, Pallas kernels, per_device(): pl.pallas_call(finish, out_shape=(jax.ShapeDtypeStruct((B, KS), F32), jax...  1.78 us

profile of v3, /device:TPU:1, one launch (start us, length us, event | category | flops | bytes accessed | tf_op | source)
XLA Modules:
  0.0 64.7 jit_solution(17237755311160893069)
XLA Ops:
  0.6 62.3 %shard_map.59 = (f32[32,1024]{1,0:T(8,128)}, f32[32,2048]{1,0:T(8,128)}) custom-call(f32[1024,2048]{1,0:T(8,128)} %e_hbm.1, s32[8,128]{1,0:T(8,128)} %bitcast.1, s32[32,2048]{1,0:T(8,128)} %counts_hbm.1, f32[32,1024]{1,0:T(8,128)} %initial_hbm.1), custom_call_target="tpu_custom_call" | custom-call | tf_op jit(solution)/shard_map/pallas_call | solution.py:341
  62.9 1.8 %shard_map.60 = (f32[32,1024]{1,0:T(8,128)}, f32[32,2048]{1,0:T(8,128)}) custom-call(f32[32,1024]{1,0:T(8,128)} %get-tuple-element.4.free_in, f32[32,2048]{1,0:T(8,128)} %get-tuple-element.5.lw_in), custom_call_target="tpu_custom_call" | custom-call | tf_op jit(solution)/shard_map/pallas_call | solution.py:380

commit v4 on v3

--- a/solution.py
+++ b/solution.py
@@ -15,6 +15,7 @@
 PIECES = 8
 W = NS // PIECES
 PAIRS = PIECES // 2
+HELD = 1
 DEEP = 256
 GROUP = 8
 RING = 8
@@ -107,6 +108,10 @@
             for k in range(3):
                 row_copies(t, k).wait_send()
 
+    def send_rows(t):
+        for k in (2, 0, 1):
+            row_copies(t, k).start()
+
     row_base = take(3 * PAIRS)
 
     small[0].wait()
@@ -127,9 +132,6 @@
         if it > 0:
             line = line + to_row(jnp.where(y == 0, val_got[it - 1, 0, :, 0:1], jnp.zeros((B, 1), F32)), B)
         ext[it] = line
-        if it == 0:
-            pl.semaphore_wait(barrier, 3 + GROUP - 1 + RING - 1)
-        ext_copies = [send(ext.at[it], ext_got.at[it, k], c, peers[k]) for k in (2, 0, 1)]
         base1, base2 = take(PIECES), take(PIECES)
 
         def copy1(p, k):
@@ -145,8 +147,7 @@
                     copy1(2 * t + k, k).wait_send()
                     copy2(2 * t + k, k).wait_send()
 
-        @pl.loop(0, PAIRS)
-        def _(t):
+        def products(t, sending):
             leasts = []
             if it == 0:
                 for k in range(2):
@@ -162,8 +163,8 @@
                     rows[t, 0:1, cols] = -least
                     rows[t, 1:2, cols] = jnp.where(y == 0, e_buf[p, 0:1, :], jnp.zeros((1, W), F32))
                     leasts.append(least)
-                for k in (2, 0, 1):
-                    row_copies(t, k).start()
+                if sending:
+                    send_rows(t)
             for k in range(2):
                 p = 2 * t + k
                 if it == 0:
@@ -182,7 +183,32 @@
                     both = jnp.dot(lhs[...], bh[p], preferred_element_type=F32)
                     rest = jnp.dot(lhs[0:B, :], bl[p], preferred_element_type=F32)
                     part1[it, p] = both[0:B] + (both[B : 2 * B] + rest)
-                copy1(p, k).start()
+                if sending:
+                    copy1(p, k).start()
+
+        held = HELD if it == 0 else 0
+        if held:
+
+            @pl.loop(0, held)
+            def _(t):
+                products(t, False)
+
+        if it == 0:
+            pl.semaphore_wait(barrier, 3 + GROUP - 1 + RING - 1)
+        ext_copies = [send(ext.at[it], ext_got.at[it, k], c, peers[k]) for k in (2, 0, 1)]
+        if held:
+
+            @pl.loop(0, held)
+            def _(t):
+                send_rows(t)
+                for k in range(2):
+                    copy1(2 * t + k, k).start()
+
+        if held < PAIRS:
+
+            @pl.loop(held, PAIRS)
+            def _(t):
+                products(t, True)
 
         for copy in ext_copies:
             copy.wait_recv()

time: 64.8 us -> 64.1 us (0.989)
  Pallas kernels: 64.1 us -> 63.3 us
    pallas_call x1, Pallas kernels: 62.3 us -> 61.5 us  [per_device(): pl.pallas_call(kernel, out_shape=tuple((jax.ShapeDtypeStruct((B, n), F32)...]
where the time goes in v4:
time: 64.1 us; the launch traced here: 64 us
  Pallas kernels  63.3 us (99%)
    pallas_call x1, Pallas kernels, per_device(): pl.pallas_call(kernel, out_shape=tuple((jax.ShapeDtypeStruct((B, n), F32)...  61.5 us
    pallas_call x1, Pallas kernels, per_device(): pl.pallas_call(finish, out_shape=(jax.ShapeDtypeStruct((B, KS), F32), jax...  1.78 us

profile of v4, /device:TPU:1, one launch (start us, length us, event | category | flops | bytes accessed | tf_op | source)
XLA Modules:
  0.0 64.0 jit_solution(17644816760322179928)
XLA Ops:
  0.6 61.5 %shard_map.59 = (f32[32,1024]{1,0:T(8,128)}, f32[32,2048]{1,0:T(8,128)}) custom-call(f32[1024,2048]{1,0:T(8,128)} %e_hbm.1, s32[8,128]{1,0:T(8,128)} %bitcast.1, s32[32,2048]{1,0:T(8,128)} %counts_hbm.1, f32[32,1024]{1,0:T(8,128)} %initial_hbm.1), custom_call_target="tpu_custom_call" | custom-call | tf_op jit(solution)/shard_map/pallas_call | solution.py:367
  62.2 1.8 %shard_map.60 = (f32[32,1024]{1,0:T(8,128)}, f32[32,2048]{1,0:T(8,128)}) custom-call(f32[32,1024]{1,0:T(8,128)} %get-tuple-element.4.free_in, f32[32,2048]{1,0:T(8,128)} %get-tuple-element.5.lw_in), custom_call_target="tpu_custom_call" | custom-call | tf_op jit(solution)/shard_map/pallas_call | solution.py:406

commit v5 on v4

--- a/solution.py
+++ b/solution.py
@@ -52,16 +52,6 @@
     z, g = c // GROUP, c % GROUP
     peers = (y + 1 - 2 * (y % 2), 3 - y, (y + 2) % 4)
 
-    barrier = pltpu.get_barrier_semaphore()
-    for peer in peers:
-        pl.semaphore_signal(barrier, inc=1, device_id={"conf": c, "state": peer}, device_id_type=MESH)
-    for o in range(1, GROUP):
-        peer = z * GROUP + (g + o) % GROUP
-        pl.semaphore_signal(barrier, inc=1, device_id={"conf": peer, "state": y}, device_id_type=MESH)
-    for o in range(1, RING):
-        peer = ((z + o) % RING) * GROUP + g
-        pl.semaphore_signal(barrier, inc=1, device_id={"conf": peer, "state": y}, device_id_type=MESH)
-
     small = [
         pltpu.make_async_copy(samples_hbm, samples, small_sem.at[0]),
         pltpu.make_async_copy(initial_hbm, lifted, small_sem.at[1]),
@@ -73,6 +63,16 @@
     for copy in loads:
         copy.start()
     small[2].start()
+
+    barrier = pltpu.get_barrier_semaphore()
+    for peer in peers:
+        pl.semaphore_signal(barrier, inc=1, device_id={"conf": c, "state": peer}, device_id_type=MESH)
+    for o in range(1, GROUP):
+        peer = z * GROUP + (g + o) % GROUP
+        pl.semaphore_signal(barrier, inc=1, device_id={"conf": peer, "state": y}, device_id_type=MESH)
+    for o in range(1, RING):
+        peer = ((z + o) % RING) * GROUP + g
+        pl.semaphore_signal(barrier, inc=1, device_id={"conf": peer, "state": y}, device_id_type=MESH)
 
     def remote(src, dst, conf, state, n):
         return pltpu.make_async_remote_copy(
@@ -183,8 +183,10 @@
                     both = jnp.dot(lhs[...], bh[p], preferred_element_type=F32)
                     rest = jnp.dot(lhs[0:B, :], bl[p], preferred_element_type=F32)
                     part1[it, p] = both[0:B] + (both[B : 2 * B] + rest)
-                if sending:
-                    copy1(p, k).start()
+
+            if sending:
+                for k in range(2):
+                    copy1(2 * t + k, k).start()
 
         held = HELD if it == 0 else 0
         if held:
@@ -258,7 +260,9 @@
             if last:
                 e0 = rows[t, 1:2, cols] + rows_got[0, t, 1:2, cols] + rows_got[1, t, 1:2, cols] + rows_got[2, t, 1:2, cols]
                 first_boltz = jnp.exp(-e0 - m)
-            copy2(p, k).wait_recv()
+            if k == 0:
+                copy2(p, 0).wait_recv()
+                copy2(p + 1, 1).wait_recv()
             denom = part2[it, p] * a + got2[it, p] * b
             ratio = weight / denom
             high, low = split(ratio * own_scale)
@@ -270,11 +274,12 @@
                 first_total = first_total + (first_terms[:, :128] + first_terms[:, 128:])
             return first_total
 
-        def terms(p, k, x):
+        def terms(t, x):
             at = pl.ds(pl.multiple_of(x * 256, 256), 256)
-            both = lax.dot_general(rhs[k], bh[p, at, :], dims, preferred_element_type=F32)
-            rest = lax.dot_general(rhs[k, 0:B, :], bl[p, at, :], dims, preferred_element_type=F32)
-            made = both[0:B] + (both[B : 2 * B] + rest)
+            both = [lax.dot_general(rhs[k], bh[2 * t + k, at, :], dims, preferred_element_type=F32) for k in range(2)]
+            rest = [lax.dot_general(rhs[k, 0:B, :], bl[2 * t + k, at, :], dims, preferred_element_type=F32) for k in range(2)]
+            made = both[0] + both[1]
+            made = made[0:B] + (made[B : 2 * B] + (rest[0] + rest[1]))
             for core in range(2):
                 j = 2 * x + core
                 tot[it, j, 0:B, :] = tot[it, j, 0:B, :] + made[:, 128 * core : 128 * (core + 1)]
@@ -282,15 +287,13 @@
         def both_pieces(t, first_total):
             for k in range(2):
                 first_total = ratios(t, k, first_total)
-                for x in range(GROUP // 2):
-                    terms(2 * t + k, k, x)
+            for x in range(GROUP // 2):
+                terms(t, x)
             return first_total
 
         first_total = lax.fori_loop(0, PAIRS - 1, both_pieces, jnp.zeros((B, 128), F32))
-        first_total = ratios(PAIRS - 1, 0, first_total)
-        for x in range(GROUP // 2):
-            terms(PIECES - 2, 0, x)
-        first_total = ratios(PAIRS - 1, 1, first_total)
+        for k in range(2):
+            first_total = ratios(PAIRS - 1, k, first_total)
 
         height = B + 1 if last else B
         span = pl.ds(0, height)
@@ -301,16 +304,13 @@
         scatter = []
         for ox in (2, 1, 3, 0):
             x = (g // 2 + ox) % (GROUP // 2)
-            terms(PIECES - 1, 1, x)
+            terms(PAIRS - 1, x)
             for oc in (0, 1):
                 if ox == 0 and oc == 0:
                     continue
                 slot = 2 * ox + oc
                 to = 2 * x + (g + oc) % 2
                 scatter.append((slot, send(tot.at[it, to, span], tot_got.at[it, slot, span], z * GROUP + to, y)))
-        if it == 0:
-            wait_rows()
-        wait_parts()
         acc = tot[it, g, 0:height, :]
         for slot, copy in scatter[::-1]:
             copy.wait_recv()
@@ -320,6 +320,9 @@
         for o in (4, 3, 5, 2, 6, 1, 7):
             around.append(send(ring.at[it, span], ring_got.at[it, z, span], ((z + o) % RING) * GROUP + g, y))
         ring_got[it, z, 0:height, :] = acc
+        if it == 0:
+            wait_rows()
+        wait_parts()
         drain()
         if last:
 

time: 64.1 us -> 63.6 us (level)
  no operation moved by 1% of the time
where the time goes in v5:
time: 63.6 us; the launch traced here: 63.5 us
  Pallas kernels  62.8 us (99%)
  between operations  0.64 us (1%)
    pallas_call x1, Pallas kernels, per_device(): pl.pallas_call(kernel, out_shape=tuple((jax.ShapeDtypeStruct((B, n), F32)...  61.1 us
    pallas_call x1, Pallas kernels, per_device(): pl.pallas_call(finish, out_shape=(jax.ShapeDtypeStruct((B, KS), F32), jax...  1.78 us

profile of v5, /device:TPU:1, one launch (start us, length us, event | category | flops | bytes accessed | tf_op | source)
XLA Modules:
  0.0 63.5 jit_solution(1333231196870451454)
XLA Ops:
  0.6 61.1 %shard_map.59 = (f32[32,1024]{1,0:T(8,128)}, f32[32,2048]{1,0:T(8,128)}) custom-call(f32[1024,2048]{1,0:T(8,128)} %e_hbm.1, s32[8,128]{1,0:T(8,128)} %bitcast.1, s32[32,2048]{1,0:T(8,128)} %counts_hbm.1, f32[32,1024]{1,0:T(8,128)} %initial_hbm.1), custom_call_target="tpu_custom_call" | custom-call | tf_op jit(solution)/shard_map/pallas_call | solution.py:370
  61.7 1.8 %shard_map.60 = (f32[32,1024]{1,0:T(8,128)}, f32[32,2048]{1,0:T(8,128)}) custom-call(f32[32,1024]{1,0:T(8,128)} %get-tuple-element.4.free_in, f32[32,2048]{1,0:T(8,128)} %get-tuple-element.5.lw_in), custom_call_target="tpu_custom_call" | custom-call | tf_op jit(solution)/shard_map/pallas_call | solution.py:409

commit v6 on v5

--- a/solution.py
+++ b/solution.py
@@ -65,14 +65,14 @@
     small[2].start()
 
     barrier = pltpu.get_barrier_semaphore()
-    for peer in peers:
-        pl.semaphore_signal(barrier, inc=1, device_id={"conf": c, "state": peer}, device_id_type=MESH)
-    for o in range(1, GROUP):
+    for o in (4, 3, 5, 2, 6, 1, 7):
+        peer = ((z + o) % RING) * GROUP + g
+        pl.semaphore_signal(barrier, inc=1, device_id={"conf": peer, "state": y}, device_id_type=MESH)
+    for o in (4, 5, 2, 3, 6, 7, 1):
         peer = z * GROUP + (g + o) % GROUP
         pl.semaphore_signal(barrier, inc=1, device_id={"conf": peer, "state": y}, device_id_type=MESH)
-    for o in range(1, RING):
-        peer = ((z + o) % RING) * GROUP + g
-        pl.semaphore_signal(barrier, inc=1, device_id={"conf": peer, "state": y}, device_id_type=MESH)
+    for peer in peers[::-1]:
+        pl.semaphore_signal(barrier, inc=1, device_id={"conf": c, "state": peer}, device_id_type=MESH)
 
     def remote(src, dst, conf, state, n):
         return pltpu.make_async_remote_copy(
@@ -311,6 +311,9 @@
                 slot = 2 * ox + oc
                 to = 2 * x + (g + oc) % 2
                 scatter.append((slot, send(tot.at[it, to, span], tot_got.at[it, slot, span], z * GROUP + to, y)))
+        if it == 0:
+            wait_rows()
+        wait_parts()
         acc = tot[it, g, 0:height, :]
         for slot, copy in scatter[::-1]:
             copy.wait_recv()
@@ -320,9 +323,6 @@
         for o in (4, 3, 5, 2, 6, 1, 7):
             around.append(send(ring.at[it, span], ring_got.at[it, z, span], ((z + o) % RING) * GROUP + g, y))
         ring_got[it, z, 0:height, :] = acc
-        if it == 0:
-            wait_rows()
-        wait_parts()
         drain()
         if last:
 

time: 63.6 us -> 63.4 us (level)
  no operation moved by 1% of the time
where the time goes in v6:
time: 63.4 us; the launch traced here: 63.3 us
  Pallas kernels  62.7 us (99%)
  between operations  0.64 us (1%)
    pallas_call x1, Pallas kernels, per_device(): pl.pallas_call(kernel, out_shape=tuple((jax.ShapeDtypeStruct((B, n), F32)...  60.9 us
    pallas_call x1, Pallas kernels, per_device(): pl.pallas_call(finish, out_shape=(jax.ShapeDtypeStruct((B, KS), F32), jax...  1.78 us

profile of v6, /device:TPU:1, one launch (start us, length us, event | category | flops | bytes accessed | tf_op | source)
XLA Modules:
  0.0 63.3 jit_solution(2456210368669473039)
XLA Ops:
  0.6 60.9 %shard_map.59 = (f32[32,1024]{1,0:T(8,128)}, f32[32,2048]{1,0:T(8,128)}) custom-call(f32[1024,2048]{1,0:T(8,128)} %e_hbm.1, s32[8,128]{1,0:T(8,128)} %bitcast.1, s32[32,2048]{1,0:T(8,128)} %counts_hbm.1, f32[32,1024]{1,0:T(8,128)} %initial_hbm.1), custom_call_target="tpu_custom_call" | custom-call | tf_op jit(solution)/shard_map/pallas_call | solution.py:370
  61.5 1.8 %shard_map.60 = (f32[32,1024]{1,0:T(8,128)}, f32[32,2048]{1,0:T(8,128)}) custom-call(f32[32,1024]{1,0:T(8,128)} %get-tuple-element.4.free_in, f32[32,2048]{1,0:T(8,128)} %get-tuple-element.5.lw_in), custom_call_target="tpu_custom_call" | custom-call | tf_op jit(solution)/shard_map/pallas_call | solution.py:409

commit v7 on v6

--- a/solution.py
+++ b/solution.py
@@ -357,9 +357,17 @@
     drain()
 
 
-def finish(free_in, lw_in, free_out, lw_out):
-    free_out[...] = free_in[...]
-    lw_out[...] = lw_in[...]
+def finish(free_in, lw_in, free_out, lw_out, free_buf, lw_buf, sem):
+    steps = []
+    for n, (src, buf, dst) in enumerate(((lw_in, lw_buf, lw_out), (free_in, free_buf, free_out))):
+        steps.append((pltpu.make_async_copy(src, buf, sem.at[2 * n]), pltpu.make_async_copy(buf, dst, sem.at[2 * n + 1])))
+    for come, _ in steps:
+        come.start()
+    for come, go in steps:
+        come.wait()
+        go.start()
+    for _, go in steps:
+        go.wait()
 
 
 def per_device(energies, samples, counts, initial):
@@ -409,8 +417,9 @@
     return pl.pallas_call(
         finish,
         out_shape=(jax.ShapeDtypeStruct((B, KS), F32), jax.ShapeDtypeStruct((B, NS), F32)),
-        in_specs=[inside] * 2,
-        out_specs=(inside,) * 2,
+        in_specs=[outside] * 2,
+        out_specs=(outside,) * 2,
+        scratch_shapes=[vmem((B, KS), F32), vmem((B, NS), F32), pltpu.SemaphoreType.DMA((4,))],
     )(free, log_weight)
 
 

time: 63.4 us -> 63.4 us (level)
  no operation moved by 1% of the time
where the time goes in v7:
time: 63.4 us; the launch traced here: 63.3 us
  Pallas kernels  62.6 us (99%)
  between operations  0.64 us (1%)
    pallas_call x1, Pallas kernels, per_device(): pl.pallas_call(kernel, out_shape=tuple((jax.ShapeDtypeStruct((B, n), F32)...  60.9 us
    pallas_call x1, Pallas kernels, per_device(): pl.pallas_call(finish, out_shape=(jax.ShapeDtypeStruct((B, KS), F32), jax...  1.73 us

profile of v7, /device:TPU:1, one launch (start us, length us, event | category | flops | bytes accessed | tf_op | source)
XLA Modules:
  0.0 63.3 jit_solution(7328224506413159490)
XLA Ops:
  0.6 60.9 %shard_map.59 = (f32[32,1024]{1,0:T(8,128)}, f32[32,2048]{1,0:T(8,128)}) custom-call(f32[1024,2048]{1,0:T(8,128)} %e_hbm.1, s32[8,128]{1,0:T(8,128)} %bitcast.1, s32[32,2048]{1,0:T(8,128)} %counts_hbm.1, f32[32,1024]{1,0:T(8,128)} %initial_hbm.1), custom_call_target="tpu_custom_call" | custom-call | tf_op jit(solution)/shard_map/pallas_call | solution.py:378
  61.5 1.7 %shard_map.60 = (f32[32,1024]{1,0:T(8,128)}, f32[32,2048]{1,0:T(8,128)}) custom-call(f32[32,1024]{1,0:T(8,128)} %get-tuple-element.4.free_in, f32[32,2048]{1,0:T(8,128)} %get-tuple-element.5.lw_in), custom_call_target="tpu_custom_call" | custom-call | tf_op jit(solution)/shard_map/pallas_call | solution.py:417
